TPU v7x, 32 devices: a whole 2x2x4 slice. The times are simulated.
32 devices in a mesh: dp: 2 (over y), tm: 16 (over z, x, core).
Axes of the slice: x: 2, y: 2, z: 4, core: 2. Of those that a mesh axis runs over, the one named last changes fastest.
Arguments:
- signal: bfloat16 [2, 16384, 256], P('dp', 'tm'), may hold values from -6 to 6
- cotangent: bfloat16 [2, 16384, 256], P('dp', 'tm'), may hold values from -6 to 6
- first_history_weight: bfloat16 [256, 512], replicated, may hold values from -0.25 to 0.25
- first_current_weight: bfloat16 [256, 512], replicated, may hold values from -0.25 to 0.25
- first_residual_weight: bfloat16 [256, 256], replicated, may hold values from -0.375 to 0.375
- second_history_weight: bfloat16 [256, 512], replicated, may hold values from -0.25 to 0.25
- second_current_weight: bfloat16 [256, 512], replicated, may hold values from -0.25 to 0.25
- second_residual_weight: bfloat16 [256, 256], replicated, may hold values from -0.375 to 0.375
Outputs:
- grad_signal: bfloat16 [2, 16384, 256], P('dp', 'tm')
- grad_past_one: bfloat16 [256, 512], replicated
- grad_now_one: bfloat16 [256, 512], replicated
- grad_mix_one: bfloat16 [256, 256], replicated
- grad_past_two: bfloat16 [256, 512], replicated
- grad_now_two: bfloat16 [256, 512], replicated
- grad_mix_two: bfloat16 [256, 256], replicated
All inputs are finite; a program needn't handle non-finite values.
Results may differ from a plain program's by a relative error of at most 0.0068.
Values may be sent and summed in bfloat16 or wider, within the bound.
A program may use at most 64 MiB of HBM per device.

v0:
```python
import math

import jax
import jax.numpy as jnp
from jax import lax
from jax.sharding import PartitionSpec as P

FIRST_DILATION = 512
SECOND_DILATION = 8192


def shifted(value, axis, steps):
    count = lax.axis_size(axis)
    leading, last = (max(0, -steps), min(count, count - steps))
    return lax.ppermute(value, axis, [(source, source + steps) for source in range(leading, last)])


def forward_layer(input_traces, past_rows, tap_past, tap_now, mixing):
    channels = input_traces.shape[-1]
    flat_now = input_traces.reshape(-1, channels)
    flat_past = past_rows.reshape(-1, channels)
    pre_act = jnp.dot(flat_past, tap_past, preferred_element_type=jnp.float32) + jnp.dot(
        flat_now, tap_now, preferred_element_type=jnp.float32
    )
    half_width = pre_act.shape[1] // 2
    filter_part = jnp.tanh(pre_act[:, :half_width])
    gate_part = jax.nn.sigmoid(pre_act[:, half_width:])
    hidden = (filter_part * gate_part).astype(jnp.bfloat16)
    output = (
        flat_now.astype(jnp.float32) + jnp.dot(hidden, mixing, preferred_element_type=jnp.float32)
    ).astype(jnp.bfloat16)
    return (filter_part, gate_part, hidden, output.reshape(input_traces.shape))


def backward_layer(input_traces, past_rows, saved, incoming_gradient, tap_past, tap_now, mixing):
    filter_part, gate_part, hidden, output = saved
    channels = input_traces.shape[-1]
    flat_now = input_traces.reshape(-1, channels)
    flat_past = past_rows.reshape(-1, channels)
    flat_up = incoming_gradient.reshape(-1, channels)
    hidden_grad = jnp.dot(flat_up, mixing.T, preferred_element_type=jnp.float32)
    filter_grad = hidden_grad * gate_part * (1.0 - filter_part * filter_part)
    gate_grad = hidden_grad * filter_part * gate_part * (1.0 - gate_part)
    pre_grad = jnp.concatenate([filter_grad, gate_grad], axis=1).astype(jnp.bfloat16)
    past_term = jnp.einsum("rc,rg->cg", flat_past, pre_grad, preferred_element_type=jnp.float32)
    now_term = jnp.einsum("rc,rg->cg", flat_now, pre_grad, preferred_element_type=jnp.float32)
    mix_term = jnp.einsum("rh,rc->hc", hidden, flat_up, preferred_element_type=jnp.float32)
    ahead_rows = (
        jnp.dot(pre_grad, tap_past.T, preferred_element_type=jnp.float32)
        .astype(jnp.bfloat16)
        .reshape(input_traces.shape)
    )
    local_grad = (
        flat_up.astype(jnp.float32)
        + jnp.dot(pre_grad, tap_now.T, preferred_element_type=jnp.float32)
    ).reshape(input_traces.shape)
    return (local_grad, ahead_rows, (past_term, now_term, mix_term))


def reduce_grads(term_list, scale_factor):
    past_term, now_term, mix_term = term_list
    summed = lax.psum((past_term, now_term, mix_term), ("dp", "tm"))
    return tuple(((member * scale_factor).astype(jnp.bfloat16) for member in summed))


def body(
    signal,
    cotangent,
    first_history_weight,
    first_current_weight,
    first_residual_weight,
    second_history_weight,
    second_current_weight,
    second_residual_weight,
):
    seq_count, number_of_steps, channels = signal.shape
    rows_all = seq_count * lax.axis_size("dp") * number_of_steps * lax.axis_size("tm")
    scale_factor = 1.0 / math.sqrt(rows_all)
    final_rows = signal[:, number_of_steps - FIRST_DILATION :, :]
    received_rows = shifted(final_rows, "tm", 1)
    first_history_rows = jnp.concatenate(
        [received_rows, signal[:, : number_of_steps - FIRST_DILATION, :]], axis=1
    )
    first_layer_stash = forward_layer(
        signal,
        first_history_rows,
        first_history_weight,
        first_current_weight,
        first_residual_weight,
    )
    hidden_activation = first_layer_stash[3]
    distant_offsets = SECOND_DILATION // number_of_steps
    past_two = shifted(hidden_activation, "tm", distant_offsets)
    second_layer_stash = forward_layer(
        hidden_activation,
        past_two,
        second_history_weight,
        second_current_weight,
        second_residual_weight,
    )
    local_two, ahead_two, second_layer_terms = backward_layer(
        hidden_activation,
        past_two,
        second_layer_stash,
        cotangent,
        second_history_weight,
        second_current_weight,
        second_residual_weight,
    )
    arrived_back = shifted(ahead_two, "tm", -distant_offsets)
    hidden_gradient = (local_two + arrived_back.astype(jnp.float32)).astype(jnp.bfloat16)
    reduced_two = reduce_grads(second_layer_terms, scale_factor)
    local_one, forward_rows_first, first_layer_terms = backward_layer(
        signal,
        first_history_rows,
        first_layer_stash,
        hidden_gradient,
        first_history_weight,
        first_current_weight,
        first_residual_weight,
    )
    leading_rows = forward_rows_first[:, :FIRST_DILATION, :]
    received_head_rows = shifted(leading_rows, "tm", -1)
    trailing_later_rows = jnp.concatenate(
        [forward_rows_first[:, FIRST_DILATION:, :], received_head_rows], axis=1
    )
    grad_signal = (local_one + trailing_later_rows.astype(jnp.float32)).astype(jnp.bfloat16)
    reduced_one = reduce_grads(first_layer_terms, scale_factor)
    return (
        grad_signal,
        reduced_one[0],
        reduced_one[1],
        reduced_one[2],
        reduced_two[0],
        reduced_two[1],
        reduced_two[2],
    )


def solution(mesh):
    in_specs = (P("dp", "tm", None), P("dp", "tm", None), P(), P(), P(), P(), P(), P())
    out_specs = (P("dp", "tm", None), P(), P(), P(), P(), P(), P())
    return jax.shard_map(body, mesh=mesh, in_specs=in_specs, out_specs=out_specs, check_vma=False)
```

profile of v0, /device:TPU:1, one launch (start us, length us, event | category | flops | bytes accessed | tf_op | source)
XLA Modules:
  0.0 217.4 jit_solution(11883145581494280156)
XLA Ops:
  7.2 0.0 copy-start
  7.2 0.0 copy-start.4
  7.2 0.0 all-reduce.3.cloned.1.call-start
  7.2 1.1 fusion.28
  8.4 4.5 %collective-permute-start = (bf16[1,512,256]{2,1,0:T(8,128)(2,1)S(1)}, bf16[1,512,256]{2,1,0:T(8,128)(2,1)S(1)}, u32[]{:S(2)}, u32[]{:S(2)}) collective-permute-start(bf16[1,512,256]{2,1,0:T(8,128)(2,1)S(1)} %get-tuple-element.19), channel_id=1, source_target_pairs={{0,1},{1,2},{2,3},{3,4},{4,5},{5,6},{6,7},{7,8},{8,9},{9,10},{10,1... | collective-permute-start | bytes 786440 | tf_op jit(solution)/shard_map/ppermute | solution.py:15
  12.9 1.6 fusion.17
  14.5 1.7 collective-permute-done
  16.2 0.0 copy-done.4
  16.2 0.5 convolution_add_fusion.1
  16.7 0.0 copy-start.1
  16.7 0.0 copy-start.7
  16.7 0.0 copy-start.5
  16.7 0.4 multiply_convert_fusion.5
  17.1 0.6 copy-done.1
  17.7 0.0 copy-done.7
  17.7 0.4 fusion.1
  18.1 4.2 %collective-permute-start.1 = (bf16[1,1024,256]{2,1,0:T(8,128)(2,1)S(1)}, bf16[1,1024,256]{2,1,0:T(8,128)(2,1)S(1)}, u32[]{:S(2)}, u32[]{:S(2)}) collective-permute-start(bf16[1,1024,256]{2,1,0:T(8,128)(2,1)S(1)} %bitcast.60), channel_id=1, source_target_pairs={{0,8},{1,9},{2,10},{3,11},{4,12},{5,13},{6,14},{7,15},{16,24},{17,... | collective-permute-start | bytes 1572872 | tf_op jit(solution)/shard_map/ppermute | solution.py:15
  22.4 0.0 copy-done.5
  22.4 0.5 fusion.29
  22.9 0.0 copy-start.8
  22.9 0.0 copy-start.9
  22.9 8.4 %collective-permute-done.1 = bf16[1,1024,256]{2,1,0:T(8,128)(2,1)S(1)} collective-permute-done((bf16[1,1024,256]{2,1,0:T(8,128)(2,1)S(1)}, bf16[1,1024,256]{2,1,0:T(8,128)(2,1)S(1)}, u32[]{:S(2)}, u32[]{:S(2)}) %collective-permute-start.1) | collective-permute-done | bytes 524320 | tf_op jit(solution)/shard_map/ppermute | solution.py:15
  31.3 0.0 copy-done
  31.3 0.5 convolution_add_fusion
  31.8 0.0 copy-done.8
  31.8 0.7 multiply_convert_fusion.4
  32.6 1.3 fusion.26
  33.8 0.5 fusion.2
  34.3 1.3 collective-permute-start.2
  35.6 1.3 fusion.13
  36.9 1.3 fusion.12
  38.2 9.5 %collective-permute-done.2 = bf16[1,1024,256]{2,1,0:T(8,128)(2,1)S(1)} collective-permute-done((bf16[1,1024,256]{2,1,0:T(8,128)(2,1)S(1)}, bf16[1,1024,256]{2,1,0:T(8,128)(2,1)S(1)}, u32[]{:S(2)}, u32[]{:S(2)}) %collective-permute-start.2) | collective-permute-done | bytes 524320 | tf_op jit(solution)/shard_map/ppermute | solution.py:15
  47.6 0.5 fusion.10
  48.1 0.7 multiply_convert_fusion.2
  48.8 1.0 fusion.30
  49.8 1.3 convolution_bitcast_fusion
  51.1 1.3 fusion.22
  52.4 0.0 all-reduce.3.cloned.1.call-update
  52.4 0.0 copy-start.6
  52.4 0.5 fusion.3
  53.0 5.9 %collective-permute-start.3 = (bf16[1,512,256]{2,1,0:T(8,128)(2,1)S(1)}, bf16[1,512,256]{2,1,0:T(8,128)(2,1)S(1)}, u32[]{:S(2)}, u32[]{:S(2)}) collective-permute-start(bf16[1,512,256]{2,1,0:T(8,128)(2,1)S(1)} %get-tuple-element.18), channel_id=1, source_target_pairs={{1,0},{2,1},{3,2},{4,3},{5,4},{6,5},{7,6},{8,7},{9,8},{10,9},{11,1... | collective-permute-start | bytes 786440 | tf_op jit(solution)/shard_map/ppermute | solution.py:15
  58.9 19.4 %collective-permute-done.3 = bf16[1,512,256]{2,1,0:T(8,128)(2,1)S(1)} collective-permute-done((bf16[1,512,256]{2,1,0:T(8,128)(2,1)S(1)}, bf16[1,512,256]{2,1,0:T(8,128)(2,1)S(1)}, u32[]{:S(2)}, u32[]{:S(2)}) %collective-permute-start.3) | collective-permute-done | bytes 262176 | tf_op jit(solution)/shard_map/ppermute | solution.py:15
  78.3 1.3 fusion.11
  79.5 126.1 %all-reduce.3.cloned.1.call-done = (f32[256,512]{1,0:T(8,128)}, f32[256,512]{1,0:T(8,128)}, f32[256,256]{1,0:T(8,128)}, f32[256,512]{1,0:T(8,128)}, f32[256,512]{1,0:T(8,128)}, /*index=5*/f32[256,256]{1,0:T(8,128)}) async-done(((f32[256,512]{1,0:T(8,128)}, f32[256,512]{1,0:T(8,128)}, f32[256,256]{1,0:T(8,128)}, f32[256,512]{1,0:T(8,128)}, f32[256,512]{1,0:T(8,128)}, /*index=5*/f32[256,256]{1,0:T(8,128)}), ...) | async-done | bytes 2621456 | tf_op jit(solution)/shard_map/psum | solution.py:62
  205.6 2.2 %multiply_convert_fusion.9 = (bf16[256,512]{1,0:T(8,128)(2,1)}, bf16[256,512]{1,0:T(8,128)(2,1)}) fusion(f32[256,512]{1,0:T(8,128)} %get-tuple-element.8, f32[256,512]{1,0:T(8,128)} %get-tuple-element.7), kind=kLoop, calls=%fused_computation.46 | loop fusion | flops 524288 | bytes 1572864 | tf_op jit(solution)/shard_map/convert_element_type | solution.py:63
  207.8 1.8 multiply_convert_fusion.11
  209.6 0.0 copy-done.3
  209.6 0.9 multiply_convert_fusion.7
  (6 shorter events, 0.0 us)
Async XLA Ops:
  7.2 24.2 %copy-start = (bf16[256,512]{1,0:T(8,128)(2,1)S(1)}, bf16[256,512]{1,0:T(8,128)(2,1)}, u32[]{:S(2)}) copy-start(bf16[256,512]{1,0:T(8,128)(2,1)} %param.13) | copy-start | bytes 786436
  7.2 9.0 %copy-start.4 = (bf16[256,512]{1,0:T(8,128)(2,1)S(1)}, bf16[256,512]{1,0:T(8,128)(2,1)}, u32[]{:S(2)}) copy-start(bf16[256,512]{1,0:T(8,128)(2,1)} %param.10) | copy-start | bytes 786436
  7.2 198.4 %all-reduce.3.cloned.1.call-start = ((), (), s32[]{:S(2)}) async-start(), calls=%async_computation | async-start | bytes 5242880 | tf_op jit(solution)/shard_map/psum | solution.py:62
  8.4 7.8 %collective-permute-start = (bf16[1,512,256]{2,1,0:T(8,128)(2,1)S(1)}, bf16[1,512,256]{2,1,0:T(8,128)(2,1)S(1)}, u32[]{:S(2)}, u32[]{:S(2)}) collective-permute-start(bf16[1,512,256]{2,1,0:T(8,128)(2,1)S(1)} %get-tuple-element.19), channel_id=1, source_target_pairs={{0,1},{1,2},{2,3},{3,4},{4,5},{5,6},{6,7},{7,8},{8,9},{9,10},{10,1... | collective-permute-start | bytes 786440 | tf_op jit(solution)/shard_map/ppermute | solution.py:15
  16.7 1.0 copy-start.1
  16.7 1.1 copy-start.7
  16.7 5.7 %copy-start.5 = (bf16[256,512]{1,0:T(8,128)(2,1)S(1)}, bf16[256,512]{1,0:T(8,128)(2,1)}, u32[]{:S(2)}) copy-start(bf16[256,512]{1,0:T(8,128)(2,1)} %param.14) | copy-start | bytes 786436
  18.1 13.2 %collective-permute-start.1 = (bf16[1,1024,256]{2,1,0:T(8,128)(2,1)S(1)}, bf16[1,1024,256]{2,1,0:T(8,128)(2,1)S(1)}, u32[]{:S(2)}, u32[]{:S(2)}) collective-permute-start(bf16[1,1024,256]{2,1,0:T(8,128)(2,1)S(1)} %bitcast.60), channel_id=1, source_target_pairs={{0,8},{1,9},{2,10},{3,11},{4,12},{5,13},{6,14},{7,15},{16,24},{17,... | collective-permute-start | bytes 1572872 | tf_op jit(solution)/shard_map/ppermute | solution.py:15
  22.9 9.0 %copy-start.8 = (bf16[1,1024,256]{2,1,0:T(8,128)(2,1)S(1)}, bf16[1,1024,256]{2,1,0:T(8,128)(2,1)}, u32[]{:S(2)}) copy-start(bf16[1,1024,256]{2,1,0:T(8,128)(2,1)} %param.9) | copy-start | bytes 1572868
  22.9 9.0 %copy-start.9 = (bf16[256,256]{1,0:T(8,128)(2,1)S(1)}, bf16[256,256]{1,0:T(8,128)(2,1)}, u32[]{:S(2)}) copy-start(bf16[256,256]{1,0:T(8,128)(2,1)} %param.15) | copy-start | bytes 393220
  34.3 13.3 %collective-permute-start.2 = (bf16[1,1024,256]{2,1,0:T(8,128)(2,1)S(1)}, bf16[1,1024,256]{2,1,0:T(8,128)(2,1)S(1)}, u32[]{:S(2)}, u32[]{:S(2)}) collective-permute-start(bf16[1,1024,256]{2,1,0:T(8,128)(2,1)S(1)} %fusion.2), channel_id=1, source_target_pairs={{8,0},{9,1},{10,2},{11,3},{12,4},{13,5},{14,6},{15,7},{24,16},{25,... | collective-permute-start | bytes 1572872 | tf_op jit(solution)/shard_map/ppermute | solution.py:15
  52.4 25.8 %copy-start.6 = (bf16[256,512]{1,0:T(8,128)(2,1)S(1)}, bf16[256,512]{1,0:T(8,128)(2,1)}, u32[]{:S(2)}) copy-start(bf16[256,512]{1,0:T(8,128)(2,1)} %param.11) | copy-start | bytes 786436
  53.0 25.3 %collective-permute-start.3 = (bf16[1,512,256]{2,1,0:T(8,128)(2,1)S(1)}, bf16[1,512,256]{2,1,0:T(8,128)(2,1)S(1)}, u32[]{:S(2)}, u32[]{:S(2)}) collective-permute-start(bf16[1,512,256]{2,1,0:T(8,128)(2,1)S(1)} %get-tuple-element.18), channel_id=1, source_target_pairs={{1,0},{2,1},{3,2},{4,3},{5,4},{6,5},{7,6},{8,7},{9,8},{10,9},{11,1... | collective-permute-start | bytes 786440 | tf_op jit(solution)/shard_map/ppermute | solution.py:15
  205.6 4.0 %copy-start.2 = (f32[256,512]{1,0:T(8,128)S(1)}, f32[256,512]{1,0:T(8,128)}, u32[]{:S(2)}) copy-start(f32[256,512]{1,0:T(8,128)} %get-tuple-element.10) | copy-start | bytes 1572868
  205.6 4.0 %copy-start.3 = (f32[256,512]{1,0:T(8,128)S(1)}, f32[256,512]{1,0:T(8,128)}, u32[]{:S(2)}) copy-start(f32[256,512]{1,0:T(8,128)} %get-tuple-element.11) | copy-start | bytes 1572868
Sparse Core Ops, SparseCore 0:
  52.5 153.0 all-reduce.2
where the time goes:
time: 219 us; the launch traced here: 217 us
  waiting for transfers between devices  165 us (75%)
  starting transfers between devices  16 us (7%)
  matrix products  14.9 us (7%)
  between operations  14.2 us (6%)
  other arithmetic  5.31 us (2%)
    psum x1, waiting for transfers between devices, reduce_grads(): summed = lax.psum((past_term, now_term, mix_term), ('dp', 'tm'))  126 us
    ppermute x4, waiting for transfers between devices, shifted(): lax.ppermute(value, axis, [(source, source + steps) for source in range(l...  39 us
    ppermute x4, starting transfers between devices, shifted(): lax.ppermute(value, axis, [(source, source + steps) for source in range(l...  15.9 us
    convert_element_type x3, other arithmetic, reduce_grads(): (member * scale_factor).astype(jnp.bfloat16)  4.89 us
  transfers between devices with their start and end apart: 5, of which 5 were waited for; matrix products, arithmetic and copies ran while one was open for 3% of the time, Pallas kernels for 0%

commit v1 on v0

v1 whole, which is shorter than its diff:
```python
import functools
import math

import jax
import jax.numpy as jnp
from jax import lax
from jax.experimental import pallas as pl
from jax.experimental.pallas import tpu as pltpu
from jax.sharding import PartitionSpec as P

FIRST_DILATION = 512
SECOND_DILATION = 8192
MESH = pl.DeviceIdType.MESH
F32 = jnp.float32
BF16 = jnp.bfloat16


def mm(a, b):
    return lax.dot_general(a, b, (((1,), (0,)), ((), ())), preferred_element_type=F32)


def mm_nt(a, b):
    return lax.dot_general(a, b, (((1,), (1,)), ((), ())), preferred_element_type=F32)


def mm_tn(a, b):
    return lax.dot_general(a, b, (((0,), (0,)), ((), ())), preferred_element_type=F32)


def sigmoid(x):
    return 0.5 * jnp.tanh(0.5 * x) + 0.5


def kernel(
    count, offset, steps, chunks,
    sig, cot, p1, w1, m1, p2, w2, m2,
    gsig, tp1, tn1, tm1, tp2, tn2, tm2,
    halo, f1, g1, h1, mid, past2, ahead2, back2, pre2, hg2, loc2, ahead1, back1, loc1,
    halo_s, halo_r, mid_s, mid_r, a2_s, a2_r, a1_s, a1_r,
):
    d1 = FIRST_DILATION
    c = sig.shape[1]
    me = lax.axis_index("tm")
    has_prev, has_next = me > 0, me < count - 1
    has_far, has_near = me < count - offset, me >= offset
    nxt, prv = lax.rem(me + 1, count), lax.rem(me + count - 1, count)
    far, near = lax.rem(me + offset, count), lax.rem(me + count - offset, count)

    barrier = pltpu.get_barrier_semaphore()
    for there, target in ((has_prev, prv), (has_next, nxt), (has_far, far), (has_near, near)):
        @pl.when(there)
        def _(target=target):
            pl.semaphore_signal(barrier, inc=1, device_id={"tm": target}, device_id_type=MESH)
    peers = sum(there.astype(jnp.int32) for there in (has_prev, has_next, has_far, has_near))
    pl.semaphore_wait(barrier, peers)

    def copy(src, dst, s, r, target):
        return pltpu.make_async_remote_copy(
            src_ref=src, dst_ref=dst, send_sem=s, recv_sem=r, device_id={"tm": target}, device_id_type=MESH
        )

    halo_copy = copy(sig.at[pl.ds(steps - d1, d1)], halo, halo_s, halo_r, nxt)
    mid_copy, a2_copy, a1_copy = [], [], []
    for i, (at, size) in enumerate(chunks):
        rows = pl.ds(at, size)
        mid_copy.append(copy(mid.at[rows], past2.at[rows], mid_s.at[i], mid_r.at[i], far))
        a2_copy.append(copy(ahead2.at[rows], back2.at[rows], a2_s.at[i], a2_r.at[i], near))
        a1_copy.append(copy(ahead1.at[rows], back1.at[rows], a1_s.at[i], a1_r.at[i], prv) if at < d1 else None)

    @pl.when(has_next)
    def _():
        halo_copy.start()

    @pl.when(jnp.logical_not(has_prev))
    def _():
        halo[...] = jnp.zeros_like(halo)

    @pl.when(jnp.logical_not(has_near))
    def _():
        past2[...] = jnp.zeros_like(past2)

    @pl.when(jnp.logical_not(has_far))
    def _():
        back2[...] = jnp.zeros_like(back2)

    @pl.when(jnp.logical_not(has_next))
    def _():
        back1[...] = jnp.zeros_like(back1)

    def past1(at, size):
        return halo[pl.ds(at, size), :] if at < d1 else sig[pl.ds(at - d1, size), :]

    def add(ref, first, value):
        ref[...] = value if first else ref[...] + value

    waited_halo = False
    for i, (at, size) in enumerate(chunks):
        rows = pl.ds(at, size)
        if at < d1 and not waited_halo:
            waited_halo = True

            @pl.when(has_prev)
            def _():
                halo_copy.wait_recv()
        u = sig[rows, :]
        pre = mm(past1(at, size), p1[...]) + mm(u, w1[...])
        f = jnp.tanh(pre[:, :c])
        g = sigmoid(pre[:, c:])
        hid = (f * g).astype(BF16)
        f1[rows, :] = f
        g1[rows, :] = g
        h1[rows, :] = hid
        mid[rows, :] = (u.astype(F32) + mm(hid, m1[...])).astype(BF16)

        @pl.when(has_far)
        def _(i=i):
            mid_copy[i].start()

    for at, size in chunks:
        rows = pl.ds(at, size)
        pre2[rows, :] = mm(mid[rows, :], w2[...])
        hg2[rows, :] = mm_nt(cot[rows, :], m2[...])

    def second(i):
        at, size = chunks[i]
        rows = pl.ds(at, size)

        @pl.when(has_near)
        def _():
            mid_copy[i].wait_recv()
        past = past2[rows, :]
        up = cot[rows, :]
        pre = mm(past, p2[...]) + pre2[rows, :]
        f = jnp.tanh(pre[:, :c])
        g = sigmoid(pre[:, c:])
        hid = (f * g).astype(BF16)
        hg = hg2[rows, :]
        pg = jnp.concatenate([hg * g * (1.0 - f * f), hg * f * g * (1.0 - g)], axis=1).astype(BF16)

        @pl.when(has_near)
        def _():
            ahead2[rows, :] = mm_nt(pg, p2[...]).astype(BF16)
            a2_copy[i].start()
        loc2[rows, :] = up.astype(F32) + mm_nt(pg, w2[...])
        add(tp2, i == 0, mm_tn(past, pg))
        add(tn2, i == 0, mm_tn(mid[rows, :], pg))
        add(tm2, i == 0, mm_tn(hid, up))

    def first(i):
        at, size = chunks[i]
        rows = pl.ds(at, size)

        @pl.when(has_far)
        def _():
            a2_copy[i].wait_recv()
        up = (loc2[rows, :] + back2[rows, :].astype(F32)).astype(BF16)
        hg = mm_nt(up, m1[...])
        f, g = f1[rows, :], g1[rows, :]
        pg = jnp.concatenate([hg * g * (1.0 - f * f), hg * f * g * (1.0 - g)], axis=1).astype(BF16)
        ahead1[rows, :] = mm_nt(pg, p1[...]).astype(BF16)
        if at < d1:
            @pl.when(has_prev)
            def _():
                a1_copy[i].start()
        loc1[rows, :] = up.astype(F32) + mm_nt(pg, w1[...])
        add(tp1, i == 0, mm_tn(past1(at, size), pg))
        add(tn1, i == 0, mm_tn(sig[rows, :], pg))
        add(tm1, i == 0, mm_tn(h1[rows, :], up))

    second(0)
    for i in range(1, len(chunks)):
        second(i)
        first(i - 1)
    first(len(chunks) - 1)

    for i, (at, size) in enumerate(chunks):
        if at < d1:
            @pl.when(has_next)
            def _(i=i):
                a1_copy[i].wait_recv()
    local = steps - d1
    if local:
        gsig[pl.ds(0, local), :] = (loc1[pl.ds(0, local), :] + ahead1[pl.ds(d1, local), :].astype(F32)).astype(BF16)
    gsig[pl.ds(local, d1), :] = (loc1[pl.ds(local, d1), :] + back1[...].astype(F32)).astype(BF16)

    @pl.when(has_next)
    def _():
        halo_copy.wait_send()
    for i in range(len(chunks)):
        @pl.when(has_far)
        def _(i=i):
            mid_copy[i].wait_send()

        @pl.when(has_near)
        def _(i=i):
            a2_copy[i].wait_send()
        if a1_copy[i] is not None:
            @pl.when(has_prev)
            def _(i=i):
                a1_copy[i].wait_send()


def body(signal, cotangent, p1, w1, m1, p2, w2, m2):
    seqs, steps, c = signal.shape
    count = lax.axis_size("tm")
    gate = p1.shape[1]
    scale = 1.0 / math.sqrt(seqs * lax.axis_size("dp") * steps * count)
    chunks = ((512, 256), (0, 256), (256, 256), (768, 128), (896, 128))
    nch = len(chunks)
    vm = pl.BlockSpec(memory_space=pltpu.VMEM)
    S = jax.ShapeDtypeStruct
    dma = pltpu.SemaphoreType.DMA
    terms = [S((c, gate), F32), S((c, gate), F32), S((c, c), F32)]
    out = pl.pallas_call(
        functools.partial(kernel, count, SECOND_DILATION // steps, steps, chunks),
        out_shape=[S((steps, c), BF16)] + terms + terms,
        in_specs=[vm] * 8,
        out_specs=[vm] * 7,
        scratch_shapes=[
            pltpu.VMEM((FIRST_DILATION, c), BF16),
            pltpu.VMEM((steps, c), F32),
            pltpu.VMEM((steps, c), F32),
            pltpu.VMEM((steps, c), BF16),
            pltpu.VMEM((steps, c), BF16),
            pltpu.VMEM((steps, c), BF16),
            pltpu.VMEM((steps, c), BF16),
            pltpu.VMEM((steps, c), BF16),
            pltpu.VMEM((steps, gate), F32),
            pltpu.VMEM((steps, c), F32),
            pltpu.VMEM((steps, c), F32),
            pltpu.VMEM((steps, c), BF16),
            pltpu.VMEM((FIRST_DILATION, c), BF16),
            pltpu.VMEM((steps, c), F32),
            dma, dma,
            dma((nch,)), dma((nch,)), dma((nch,)), dma((nch,)), dma((nch,)), dma((nch,)),
        ],
        compiler_params=pltpu.CompilerParams(
            collective_id=0, has_side_effects=True, vmem_limit_bytes=48 * 1024 * 1024
        ),
        name="layers",
    )(signal.reshape(steps, c), cotangent.reshape(steps, c), p1, w1, m1, p2, w2, m2)
    summed = lax.psum(tuple(out[1:]), ("dp", "tm"))
    grads = tuple((t * scale).astype(BF16) for t in summed)
    return (out[0].reshape(signal.shape),) + grads


def solution(mesh):
    in_specs = (P("dp", "tm", None), P("dp", "tm", None), P(), P(), P(), P(), P(), P())
    out_specs = (P("dp", "tm", None), P(), P(), P(), P(), P(), P())
    return jax.shard_map(body, mesh=mesh, in_specs=in_specs, out_specs=out_specs, check_vma=False)
```

time: 219 us -> 210 us (0.959)
  Pallas kernels: 0 us -> 29.8 us
  starting transfers between devices: 16 us -> 0.04 us
  matrix products: 14.9 us -> 0 us
  waiting for transfers between devices: 165 us -> 151 us
  local copies, waits for them, and re-layouts: 1.82 us -> 8.86 us
    ppermute x4 -> x0, waiting for transfers between devices: 39 us -> none  [shifted(): lax.ppermute(value, axis, [(source, source + steps) for source in range(l...]
    pallas_call x0 -> x1, Pallas kernels: none -> 29.8 us  [body(): pl.pallas_call(functools.partial(kernel, count, SECOND_DILATION // steps,...]
    psum x1, waiting for transfers between devices: 126 us -> 151 us  [body(): summed = lax.psum(tuple(out[1:]), ('dp', 'tm'))]
    ppermute x4 -> x0, starting transfers between devices: 15.9 us -> none  [shifted(): lax.ppermute(value, axis, [(source, source + steps) for source in range(l...]
    dot_general x17 -> x0, matrix products: 14.9 us -> none  [the longest x2 2.56 us: backward_layer(): jnp.einsum('rc,rg->cg', flat_now, pre_grad, preferred_element_type=jnp.fl...]
    unnamed x20 -> x25, local copies, waits for them, and re-layouts: 0.66 us -> 8.86 us
    convert_element_type x4 -> x3, other arithmetic: 5.31 us -> 3.86 us  [body(): grads = tuple(((t * scale).astype(BF16) for t in summed))]
  transfers between devices with their start and end apart: 5 -> 1, of which waited for: 5 -> 1; matrix products, arithmetic and copies ran while one was open for 3% -> 0% of each run, Pallas kernels for 0% -> 0%
where the time goes in v1:
time: 210 us; the launch traced here: 208 us
  waiting for transfers between devices  151 us (72%)
  Pallas kernels  29.8 us (14%)
  between operations  14.1 us (7%)
  local copies, waits for them, and re-layouts  8.86 us (4%)
  other arithmetic  3.86 us (2%)
    psum x1, waiting for transfers between devices, body(): summed = lax.psum(tuple(out[1:]), ('dp', 'tm'))  151 us
    pallas_call x1, Pallas kernels, body(): pl.pallas_call(functools.partial(kernel, count, SECOND_DILATION // steps,...  29.8 us
    unnamed x25, local copies, waits for them, and re-layouts  8.86 us
  transfers between devices with their start and end apart: 1, of which 1 were waited for; matrix products, arithmetic and copies ran while one was open for 0% of the time, Pallas kernels for 0%

profile of v1, /device:TPU:1, one launch (start us, length us, event | category | flops | bytes accessed | tf_op | source)
XLA Modules:
  0.0 208.0 jit_solution(4227845318633112686)
XLA Ops:
  7.2 0.0 all-reduce.3.cloned.1.call-start
  7.2 0.0 copy-start
  7.2 1.0 copy-done
  8.3 0.0 copy-start.1
  8.3 1.0 copy-done.1
  9.3 0.0 copy-start.2
  9.3 0.9 copy-done.2
  10.3 0.0 copy-start.3
  10.3 0.9 copy-done.3
  11.2 0.0 copy-start.4
  11.2 0.9 copy-done.4
  12.2 0.0 copy-start.5
  12.2 0.9 copy-done.5
  13.1 0.0 copy-start.6
  13.1 0.9 copy-done.6
  14.0 0.0 copy-start.7
  14.0 0.9 copy-done.7
  14.9 29.8 %layers.1 = (bf16[1024,256]{1,0:T(8,128)(2,1)S(1)}, f32[256,512]{1,0:T(8,128)}, f32[256,512]{1,0:T(8,128)}, f32[256,256]{1,0:T(8,128)}, f32[256,512]{1,0:T(8,128...) custom-call(bf16[1024,256]{1,0:T(8,128)(2,1)S(1)} %bitcast.4, bf16[1024,256]{1,0:T(8,128)(2,1)S(1)} %bitcast.5, ...), custom_call_target="tpu_custom_call" | custom-call | tf_op jit(solution)/shard_map/layers/pallas_call | solution.py:214
  44.7 0.0 all-reduce.3.cloned.1.call-update
  44.7 151.4 %all-reduce.3.cloned.1.call-done = (f32[256,512]{1,0:T(8,128)}, f32[256,512]{1,0:T(8,128)}, f32[256,256]{1,0:T(8,128)}, f32[256,512]{1,0:T(8,128)}, f32[256,512]{1,0:T(8,128)}, /*index=5*/f32[256,256]{1,0:T(8,128)}) async-done(((f32[256,512]{1,0:T(8,128)}, f32[256,512]{1,0:T(8,128)}, f32[256,256]{1,0:T(8,128)}, f32[256,512]{1,0:T(8,128)}, f32[256,512]{1,0:T(8,128)}, /*index=5*/f32[256,256]{1,0:T(8,128)}), ...) | async-done | bytes 2621456 | tf_op jit(solution)/shard_map/psum | solution.py:242
  196.1 0.0 copy-start.10
  196.1 0.0 copy-start.11
  196.1 0.0 copy-start.9
  196.1 2.2 %multiply_convert_fusion.2 = (bf16[256,512]{1,0:T(8,128)(2,1)}, bf16[256,512]{1,0:T(8,128)(2,1)}) fusion(f32[256,512]{1,0:T(8,128)} %get-tuple-element.22, f32[256,512]{1,0:T(8,128)} %get-tuple-element.21), kind=kLoop, calls=%fused_computation.2 | loop fusion | flops 524288 | bytes 1572864 | tf_op jit(solution)/shard_map/convert_element_type | solution.py:243
  198.3 0.0 copy-start.8
  198.3 0.0 copy-done.10
  198.3 0.0 copy-done.11
  198.3 0.7 multiply_convert_fusion.4
  199.1 0.0 copy-done.9
  199.1 0.4 copy-done.8
  199.4 0.9 multiply_convert_fusion
  200.3 0.8 copy.22
Async XLA Ops:
  7.2 188.9 %all-reduce.3.cloned.1.call-start = ((), (), s32[]{:S(2)}) async-start(), calls=%async_computation | async-start | bytes 5242880 | tf_op jit(solution)/shard_map/psum | solution.py:242
  7.2 1.0 copy-start
  8.3 1.0 copy-start.1
  9.3 0.9 copy-start.2
  10.3 0.9 copy-start.3
  11.2 0.9 copy-start.4
  12.2 0.9 copy-start.5
  13.1 0.9 copy-start.6
  14.0 0.9 copy-start.7
  196.1 2.2 %copy-start.10 = (f32[256,256]{1,0:T(8,128)S(1)}, f32[256,256]{1,0:T(8,128)}, u32[]{:S(2)}) copy-start(f32[256,256]{1,0:T(8,128)} %get-tuple-element.23) | copy-start | bytes 786436
  196.1 2.2 %copy-start.11 = (f32[256,256]{1,0:T(8,128)S(1)}, f32[256,256]{1,0:T(8,128)}, u32[]{:S(2)}) copy-start(f32[256,256]{1,0:T(8,128)} %get-tuple-element.26) | copy-start | bytes 786436
  196.1 3.0 %copy-start.9 = (f32[256,512]{1,0:T(8,128)S(1)}, f32[256,512]{1,0:T(8,128)}, u32[]{:S(2)}) copy-start(f32[256,512]{1,0:T(8,128)} %get-tuple-element.25) | copy-start | bytes 1572868
  198.3 1.1 copy-start.8
Sparse Core Ops, SparseCore 0:
  44.9 151.1 all-reduce.2

commit v2 on v1

--- a/solution.py
+++ b/solution.py
@@ -31,13 +31,145 @@
     return 0.5 * jnp.tanh(0.5 * x) + 0.5
 
 
-def kernel(
-    count, offset, steps, chunks,
-    sig, cot, p1, w1, m1, p2, w2, m2,
-    gsig, tp1, tn1, tm1, tp2, tn2, tm2,
-    halo, f1, g1, h1, mid, past2, ahead2, back2, pre2, hg2, loc2, ahead1, back1, loc1,
-    halo_s, halo_r, mid_s, mid_r, a2_s, a2_r, a1_s, a1_r,
-):
+class Sum:
+    def __init__(self, acc, pack, got1, got2, got3, sum1, sum2, res, ss, rs, scale):
+        self.acc, self.pack, self.got1, self.got2, self.got3 = acc, pack, got1, got2, got3
+        self.sum1, self.sum2, self.res, self.ss, self.rs, self.scale = sum1, sum2, res, ss, rs, scale
+        half = acc.shape[0] // 2
+        quarter, piece = half // 4, half // 16
+        self.half, self.quarter, self.piece = half, quarter, piece
+        dp, me = lax.axis_index("dp"), lax.axis_index("tm")
+        q, p, z, partner, plane, column = places(dp, me)
+        self.mine = pl.multiple_of(q * half, half)
+        self.other = pl.multiple_of((1 - q) * half, half)
+        self.base2 = pl.multiple_of(q * half + p * quarter, quarter)
+        self.base3 = pl.multiple_of(q * half + p * quarter + z * piece, piece)
+        self.own2 = pl.multiple_of(p * quarter, quarter)
+        self.own3 = pl.multiple_of(z * piece, piece)
+        sem = iter(range(14))
+
+        def copy(src, dst, target):
+            i = next(sem)
+            return pltpu.make_async_remote_copy(
+                src_ref=src, dst_ref=dst, send_sem=ss.at[i], recv_sem=rs.at[i], device_id=target, device_id_type=MESH
+            )
+
+        self.c1 = [copy(pack, got1, partner)]
+        self.c2 = []
+        for r, (there, place) in enumerate(plane):
+            rows = pl.ds(pl.multiple_of(place * quarter, quarter), quarter)
+            self.c2.append(copy(sum1.at[rows], got2.at[r], there))
+        self.c3 = []
+        for r, (there, place) in enumerate(column):
+            rows = pl.ds(pl.multiple_of(place * piece, piece), piece)
+            self.c3.append(copy(sum2.at[rows], got3.at[r], there))
+        three, two = res.at[pl.ds(self.base3, piece)], res.at[pl.ds(self.base2, quarter)]
+        one = res.at[pl.ds(self.mine, half)]
+        self.g3 = [copy(three, three, there) for there, _ in column]
+        self.g2 = [copy(two, two, there) for there, _ in plane]
+        self.g1 = [copy(one, one, partner)]
+
+    def add(self, first, past, now, mix):
+        for at, value in ((0, past), (4, now), (8, mix)):
+            if value is None:
+                continue
+            for j in range(value.shape[1] // 128):
+                rows = pl.ds((at + j) * value.shape[0], value.shape[0])
+                part = value[:, j * 128 : (j + 1) * 128]
+                self.acc[rows, :] = part if first else self.acc[rows, :] + part
+
+    def start(self, copies):
+        for c in copies:
+            c.start()
+
+    def arrive(self, copies):
+        for c in copies:
+            c.wait_recv()
+
+    def send1(self):
+        self.pack[...] = self.acc[pl.ds(self.other, self.half), :].astype(BF16)
+        self.start(self.c1)
+
+    def send2(self):
+        self.arrive(self.c1)
+        total = self.acc[pl.ds(self.mine, self.half), :] + self.got1[...].astype(F32)
+        self.acc[pl.ds(self.mine, self.half), :] = total
+        self.sum1[...] = total.astype(BF16)
+        self.start(self.c2)
+
+    def send3(self):
+        self.arrive(self.c2)
+        total = self.acc[pl.ds(self.base2, self.quarter), :]
+        for r in range(3):
+            total = total + self.got2[r].astype(F32)
+        self.acc[pl.ds(self.base2, self.quarter), :] = total
+        self.sum2[...] = total.astype(BF16)
+        self.start(self.c3)
+
+    def back3(self):
+        self.arrive(self.c3)
+        total = self.acc[pl.ds(self.base3, self.piece), :]
+        for r in range(3):
+            total = total + self.got3[r].astype(F32)
+        self.res[pl.ds(self.base3, self.piece), :] = (total * self.scale).astype(BF16)
+        self.start(self.g3)
+
+    def back2(self):
+        self.arrive(self.g3)
+        self.start(self.g2)
+
+    def back1(self):
+        self.arrive(self.g2)
+        self.start(self.g1)
+
+    def finish(self):
+        self.arrive(self.g1)
+
+    def drain(self):
+        for c in self.c1 + self.c2 + self.c3 + self.g3 + self.g2 + self.g1:
+            c.wait_send()
+
+
+class Local(Sum):
+    def __init__(self, acc):
+        self.acc = acc
+
+    def nothing(self):
+        pass
+
+    send1 = send2 = send3 = back3 = back2 = back1 = finish = drain = nothing
+
+
+def places(dp, me):
+    q, x, z = lax.rem(me, 2), lax.rem(lax.div(me, 2), 2), lax.div(me, 4)
+    z0, z1 = lax.rem(z, 2), lax.div(z, 2)
+    partner = {"dp": dp, "tm": me + 1 - 2 * q}
+    plane, column = [], []
+    for r in (1, 2, 3):
+        lo, hi = r % 2, r // 2
+        xx = x + lo * (1 - 2 * x)
+        yy = dp + hi * (1 - 2 * dp)
+        plane.append(({"dp": yy, "tm": me + 2 * (xx - x)}, yy * 2 + xx))
+        zz = z + lo * (1 - 2 * z0) + 2 * hi * (1 - 2 * z1)
+        column.append(({"dp": dp, "tm": me + 4 * (zz - z)}, zz))
+    return q, dp * 2 + x, z, partner, plane, column
+
+
+def kernel(count, offset, steps, chunks, scale, fused, *refs):
+    hbm, refs = refs[:8], refs[8:]
+    results, refs = refs[:3], refs[3:]
+    vmem, refs = refs[:8], refs[8:]
+    gsig, out1, out2, store, refs = refs[0], refs[1], refs[2], refs[3], refs[4:]
+    stores = [pltpu.make_async_copy(src, dst, store.at[i]) for i, (src, dst) in enumerate(zip((gsig, out1, out2), results))]
+    halo, f1, g1, h1, mid, past2, ahead2, back2, pre2, hg2, loc2, ahead1, back1, loc1 = refs[:14]
+    load, halo_s, halo_r, mid_s, mid_r, a2_s, a2_r, a1_s, a1_r = refs[14:23]
+    sig, cot, p1, w1, m1, p2, w2, m2 = vmem
+    loads = {}
+    for i, (src, dst) in enumerate(zip(hbm, vmem)):
+        loads[i] = pltpu.make_async_copy(src, dst, load.at[i])
+    for i in (0, 3, 2, 4, 6, 1, 7, 5):
+        loads[i].start()
+
     d1 = FIRST_DILATION
     c = sig.shape[1]
     me = lax.axis_index("tm")
@@ -47,19 +179,30 @@
     far, near = lax.rem(me + offset, count), lax.rem(me + count - offset, count)
 
     barrier = pltpu.get_barrier_semaphore()
+    peers = sum(there.astype(jnp.int32) for there in (has_prev, has_next, has_far, has_near))
     for there, target in ((has_prev, prv), (has_next, nxt), (has_far, far), (has_near, near)):
         @pl.when(there)
         def _(target=target):
             pl.semaphore_signal(barrier, inc=1, device_id={"tm": target}, device_id_type=MESH)
-    peers = sum(there.astype(jnp.int32) for there in (has_prev, has_next, has_far, has_near))
+    if fused:
+        _, _, _, partner, plane, column = places(lax.axis_index("dp"), me)
+        for target in [partner] + [there for there, _ in plane + column]:
+            pl.semaphore_signal(barrier, inc=1, device_id=target, device_id_type=MESH)
+        peers = peers + 7
     pl.semaphore_wait(barrier, peers)
+    if fused:
+        per = refs[23:]
+        sum_one = Sum(*per[:7], out1, *per[7:9], scale)
+        sum_two = Sum(*per[9:16], out2, *per[16:18], scale)
+    else:
+        sum_one, sum_two = Local(out1), Local(out2)
 
     def copy(src, dst, s, r, target):
         return pltpu.make_async_remote_copy(
             src_ref=src, dst_ref=dst, send_sem=s, recv_sem=r, device_id={"tm": target}, device_id_type=MESH
         )
 
-    halo_copy = copy(sig.at[pl.ds(steps - d1, d1)], halo, halo_s, halo_r, nxt)
+    halo_copy = copy(hbm[0].at[pl.ds(steps - d1, d1)], halo, halo_s, halo_r, nxt)
     mid_copy, a2_copy, a1_copy = [], [], []
     for i, (at, size) in enumerate(chunks):
         rows = pl.ds(at, size)
@@ -90,9 +233,8 @@
     def past1(at, size):
         return halo[pl.ds(at, size), :] if at < d1 else sig[pl.ds(at - d1, size), :]
 
-    def add(ref, first, value):
-        ref[...] = value if first else ref[...] + value
-
+    for i in (0, 3, 2, 4):
+        loads[i].wait()
     waited_halo = False
     for i, (at, size) in enumerate(chunks):
         rows = pl.ds(at, size)
@@ -116,6 +258,8 @@
         def _(i=i):
             mid_copy[i].start()
 
+    for i in (6, 1, 7, 5):
+        loads[i].wait()
     for at, size in chunks:
         rows = pl.ds(at, size)
         pre2[rows, :] = mm(mid[rows, :], w2[...])
@@ -142,9 +286,7 @@
             ahead2[rows, :] = mm_nt(pg, p2[...]).astype(BF16)
             a2_copy[i].start()
         loc2[rows, :] = up.astype(F32) + mm_nt(pg, w2[...])
-        add(tp2, i == 0, mm_tn(past, pg))
-        add(tn2, i == 0, mm_tn(mid[rows, :], pg))
-        add(tm2, i == 0, mm_tn(hid, up))
+        sum_two.add(i == 0, mm_tn(past, pg), mm_tn(mid[rows, :], pg), mm_tn(hid, up))
 
     def first(i):
         at, size = chunks[i]
@@ -157,21 +299,39 @@
         hg = mm_nt(up, m1[...])
         f, g = f1[rows, :], g1[rows, :]
         pg = jnp.concatenate([hg * g * (1.0 - f * f), hg * f * g * (1.0 - g)], axis=1).astype(BF16)
-        ahead1[rows, :] = mm_nt(pg, p1[...]).astype(BF16)
-        if at < d1:
-            @pl.when(has_prev)
-            def _():
-                a1_copy[i].start()
-        loc1[rows, :] = up.astype(F32) + mm_nt(pg, w1[...])
-        add(tp1, i == 0, mm_tn(past1(at, size), pg))
-        add(tn1, i == 0, mm_tn(sig[rows, :], pg))
-        add(tm1, i == 0, mm_tn(h1[rows, :], up))
-
+        def terms():
+            sum_one.add(i == 0, mm_tn(past1(at, size), pg), mm_tn(sig[rows, :], pg), mm_tn(h1[rows, :], up))
+
+        def grads():
+            ahead1[rows, :] = mm_nt(pg, p1[...]).astype(BF16)
+            if at < d1:
+                @pl.when(has_prev)
+                def _():
+                    a1_copy[i].start()
+            loc1[rows, :] = up.astype(F32) + mm_nt(pg, w1[...])
+
+        if i < last:
+            grads()
+            terms()
+        else:
+            terms()
+            sum_one.send1()
+            grads()
+
+    last = len(chunks) - 1
     second(0)
-    for i in range(1, len(chunks)):
+    for i in range(1, last):
         second(i)
         first(i - 1)
-    first(len(chunks) - 1)
+    second(last)
+    sum_two.send1()
+    first(last - 1)
+    sum_two.send2()
+    sum_two.send3()
+    first(last)
+    sum_two.back3()
+    sum_one.send2()
+    sum_two.back2()
 
     for i, (at, size) in enumerate(chunks):
         if at < d1:
@@ -182,6 +342,22 @@
     if local:
         gsig[pl.ds(0, local), :] = (loc1[pl.ds(0, local), :] + ahead1[pl.ds(d1, local), :].astype(F32)).astype(BF16)
     gsig[pl.ds(local, d1), :] = (loc1[pl.ds(local, d1), :] + back1[...].astype(F32)).astype(BF16)
+    stores[0].start()
+
+    sum_one.send3()
+    sum_two.back1()
+    sum_one.back3()
+    sum_one.back2()
+    sum_two.finish()
+    stores[2].start()
+    sum_one.back1()
+    sum_one.finish()
+    stores[1].start()
+    sum_one.drain()
+    sum_two.drain()
+
+    for c in stores:
+        c.wait()
 
     @pl.when(has_next)
     def _():
@@ -200,23 +376,59 @@
                 a1_copy[i].wait_send()
 
 
+def write(gs, one, two, gsig, gp1, gn1, gm1, gp2, gn2, gm2, sem):
+    copies = [pltpu.make_async_copy(gs, gsig, sem.at[20])]
+    for k, (packed, outs) in enumerate(((one, (gp1, gn1, gm1)), (two, (gp2, gn2, gm2)))):
+        block = 0
+        for out in outs:
+            height = out.shape[0]
+            for j in range(out.shape[1] // 128):
+                src = packed.at[pl.ds(block * height, height)]
+                copies.append(pltpu.make_async_copy(src, out.at[:, pl.ds(j * 128, 128)], sem.at[k * 10 + block]))
+                block += 1
+    for c in copies:
+        c.start()
+    for c in copies:
+        c.wait()
+
+
 def body(signal, cotangent, p1, w1, m1, p2, w2, m2):
     seqs, steps, c = signal.shape
-    count = lax.axis_size("tm")
+    count, groups = lax.axis_size("tm"), lax.axis_size("dp")
     gate = p1.shape[1]
-    scale = 1.0 / math.sqrt(seqs * lax.axis_size("dp") * steps * count)
+    scale = 1.0 / math.sqrt(seqs * groups * steps * count)
+    fused = (groups, count) == (2, 16)
     chunks = ((512, 256), (0, 256), (256, 256), (768, 128), (896, 128))
     nch = len(chunks)
-    vm = pl.BlockSpec(memory_space=pltpu.VMEM)
+    hbm = pl.BlockSpec(memory_space=pltpu.HBM)
     S = jax.ShapeDtypeStruct
     dma = pltpu.SemaphoreType.DMA
-    terms = [S((c, gate), F32), S((c, gate), F32), S((c, c), F32)]
-    out = pl.pallas_call(
-        functools.partial(kernel, count, SECOND_DILATION // steps, steps, chunks),
-        out_shape=[S((steps, c), BF16)] + terms + terms,
-        in_specs=[vm] * 8,
-        out_specs=[vm] * 7,
-        scratch_shapes=[
+    wide = (2 * gate + c) // 128 * c
+    packed = S((wide, 128), BF16 if fused else F32)
+    args = (signal.reshape(steps, c), cotangent.reshape(steps, c), p1, w1, m1, p2, w2, m2)
+    half = wide // 2
+    per_sum = [
+        pltpu.VMEM((wide, 128), F32),
+        pltpu.VMEM((half, 128), BF16),
+        pltpu.VMEM((half, 128), BF16),
+        pltpu.VMEM((3, half // 4, 128), BF16),
+        pltpu.VMEM((3, half // 16, 128), BF16),
+        pltpu.VMEM((half, 128), BF16),
+        pltpu.VMEM((half // 4, 128), BF16),
+        dma((14,)),
+        dma((14,)),
+    ]
+    gs, one, two = pl.pallas_call(
+        functools.partial(kernel, count, SECOND_DILATION // steps, steps, chunks, scale, fused),
+        out_shape=[S((steps, c), BF16), packed, packed],
+        in_specs=[hbm] * 8,
+        out_specs=[hbm] * 3,
+        scratch_shapes=[pltpu.VMEM(a.shape, BF16) for a in args]
+        + [
+            pltpu.VMEM((steps, c), BF16),
+            pltpu.VMEM(packed.shape, packed.dtype),
+            pltpu.VMEM(packed.shape, packed.dtype),
+            dma((3,)),
             pltpu.VMEM((FIRST_DILATION, c), BF16),
             pltpu.VMEM((steps, c), F32),
             pltpu.VMEM((steps, c), F32),
@@ -231,17 +443,30 @@
             pltpu.VMEM((steps, c), BF16),
             pltpu.VMEM((FIRST_DILATION, c), BF16),
             pltpu.VMEM((steps, c), F32),
+            dma((8,)),
             dma, dma,
             dma((nch,)), dma((nch,)), dma((nch,)), dma((nch,)), dma((nch,)), dma((nch,)),
-        ],
+        ]
+        + (per_sum * 2 if fused else []),
         compiler_params=pltpu.CompilerParams(
-            collective_id=0, has_side_effects=True, vmem_limit_bytes=48 * 1024 * 1024
+            collective_id=0, has_side_effects=True, vmem_limit_bytes=62 * 1024 * 1024
         ),
         name="layers",
-    )(signal.reshape(steps, c), cotangent.reshape(steps, c), p1, w1, m1, p2, w2, m2)
-    summed = lax.psum(tuple(out[1:]), ("dp", "tm"))
-    grads = tuple((t * scale).astype(BF16) for t in summed)
-    return (out[0].reshape(signal.shape),) + grads
+    )(*args)
+    if not fused:
+        one, two = lax.psum((one, two), ("dp", "tm"))
+        one, two = (one * scale).astype(BF16), (two * scale).astype(BF16)
+    shapes = [S((steps, c), BF16)] + [S((c, gate), BF16), S((c, gate), BF16), S((c, c), BF16)] * 2
+    out = pl.pallas_call(
+        write,
+        out_shape=shapes,
+        in_specs=[hbm] * 3,
+        out_specs=[hbm] * 7,
+        scratch_shapes=[dma((21,))],
+        compiler_params=pltpu.CompilerParams(vmem_limit_bytes=62 * 1024 * 1024),
+        name="write",
+    )(gs, one, two)
+    return (out[0].reshape(signal.shape),) + tuple(out[1:])
 
 
 def solution(mesh):

time: 210 us -> 134 us (0.64)
  waiting for transfers between devices: 151 us -> 0 us
  Pallas kernels: 29.8 us -> 133 us
  between operations: 14.1 us -> 0.64 us
  local copies, waits for them, and re-layouts: 8.86 us -> 0 us
  other arithmetic: 3.86 us -> 0 us
    psum x1 -> x0, waiting for transfers between devices: 151 us -> none  [body(): summed = lax.psum(tuple(out[1:]), ('dp', 'tm'))]
    pallas_call x0 -> x1, Pallas kernels: none -> 56.9 us  [body(): pl.pallas_call(write, out_shape=shapes, in_specs=[hbm] * 3, out_specs=[hb...]
    pallas_call x1, Pallas kernels: 29.8 us -> 76.1 us  [body(): pl.pallas_call(functools.partial(kernel, count, SECOND_DILATION // steps,...]
    unnamed x25 -> x0, local copies, waits for them, and re-layouts: 8.86 us -> none
    convert_element_type x3 -> x0, other arithmetic: 3.86 us -> none  [body(): grads = tuple(((t * scale).astype(BF16) for t in summed))]
  transfers between devices with their start and end apart: 1 -> 0, of which waited for: 1 -> 0; matrix products, arithmetic and copies ran while one was open for 0% -> 0% of each run, Pallas kernels for 0% -> 0%
where the time goes in v2:
time: 134 us
  Pallas kernels  133 us (99%)
    pallas_call x1, Pallas kernels, body(): pl.pallas_call(functools.partial(kernel, count, SECOND_DILATION // steps,...  76.1 us
    pallas_call x1, Pallas kernels, body(): pl.pallas_call(write, out_shape=shapes, in_specs=[hbm] * 3, out_specs=[hb...  56.9 us

profile of v2, /device:TPU:1, one launch (start us, length us, event | category | flops | bytes accessed | tf_op | source)
XLA Modules:
  0.0 133.6 jit_solution(7196857969899413356)
XLA Ops:
  0.6 76.1 %layers.1 = (bf16[1024,256]{1,0:T(8,128)(2,1)}, bf16[2560,128]{1,0:T(8,128)(2,1)}, bf16[2560,128]{1,0:T(8,128)(2,1)}) custom-call(bf16[1024,256]{1,0:T(8,128)(2,1)} %bitcast.3, bf16[1024,256]{1,0:T(8,128)(2,1)} %bitcast.4, bf16[256,512]{1,0:T(8,128)(2,1)} %refs_2_.1, bf16[256,512]{1,0:T(8,128)(2,1)} %refs_3_.1, bf16[256,256]{1,0:T(8,128)(2,1)} %refs_4_.1, ...), custom_call_target="tpu_custom_call" | custom-call | tf_op jit(solution)/shard_map/layers/pallas_call | solution.py:421
  76.7 56.9 %write.1 = (bf16[1024,256]{1,0:T(8,128)(2,1)}, bf16[256,512]{1,0:T(8,128)(2,1)}, bf16[256,512]{1,0:T(8,128)(2,1)}, bf16[256,256]{1,0:T(8,128)(2,1)}, bf16[256,51...) custom-call(bf16[1024,256]{1,0:T(8,128)(2,1)} %get-tuple-element.17.gs, ...), custom_call_target="tpu_custom_call" | custom-call | tf_op jit(solution)/shard_map/write/pallas_call | solution.py:460

commit v3 on v2

--- a/solution.py
+++ b/solution.py
@@ -157,10 +157,20 @@
 
 def kernel(count, offset, steps, chunks, scale, fused, *refs):
     hbm, refs = refs[:8], refs[8:]
-    results, refs = refs[:3], refs[3:]
+    results, refs = refs[:7], refs[7:]
     vmem, refs = refs[:8], refs[8:]
-    gsig, out1, out2, store, refs = refs[0], refs[1], refs[2], refs[3], refs[4:]
-    stores = [pltpu.make_async_copy(src, dst, store.at[i]) for i, (src, dst) in enumerate(zip((gsig, out1, out2), results))]
+    local, out1, out2, store, refs = refs[:7], refs[7], refs[8], refs[9], refs[10:]
+    gsig = local[0]
+    stores = [pltpu.make_async_copy(src, dst, store.at[i]) for i, (src, dst) in enumerate(zip(local, results))]
+
+    def unpack(packed, first):
+        block = 0
+        for i in range(first, first + 3):
+            height, width = local[i].shape
+            for j in range(width // 128):
+                local[i][:, j * 128 : (j + 1) * 128] = packed[pl.ds(block * height, height), :]
+                block += 1
+            stores[i].start()
     halo, f1, g1, h1, mid, past2, ahead2, back2, pre2, hg2, loc2, ahead1, back1, loc1 = refs[:14]
     load, halo_s, halo_r, mid_s, mid_r, a2_s, a2_r, a1_s, a1_r = refs[14:23]
     sig, cot, p1, w1, m1, p2, w2, m2 = vmem
@@ -235,6 +245,13 @@
 
     for i in (0, 3, 2, 4):
         loads[i].wait()
+    def send_middle(i):
+        @pl.when(has_far)
+        def _():
+            if i >= 2:
+                mid_copy[i - 2].wait_send()
+            mid_copy[i].start()
+
     waited_halo = False
     for i, (at, size) in enumerate(chunks):
         rows = pl.ds(at, size)
@@ -254,9 +271,8 @@
         h1[rows, :] = hid
         mid[rows, :] = (u.astype(F32) + mm(hid, m1[...])).astype(BF16)
 
-        @pl.when(has_far)
-        def _(i=i):
-            mid_copy[i].start()
+        if i < 2:
+            send_middle(i)
 
     for i in (6, 1, 7, 5):
         loads[i].wait()
@@ -320,13 +336,19 @@
 
     last = len(chunks) - 1
     second(0)
-    for i in range(1, last):
-        second(i)
-        first(i - 1)
-    second(last)
+    send_middle(2)
+    second(1)
+    send_middle(3)
+    second(2)
+    send_middle(4)
+    first(0)
+    second(3)
+    first(1)
+    second(4)
     sum_two.send1()
+    first(2)
+    sum_two.send2()
     first(last - 1)
-    sum_two.send2()
     sum_two.send3()
     first(last)
     sum_two.back3()
@@ -338,10 +360,10 @@
             @pl.when(has_next)
             def _(i=i):
                 a1_copy[i].wait_recv()
-    local = steps - d1
-    if local:
-        gsig[pl.ds(0, local), :] = (loc1[pl.ds(0, local), :] + ahead1[pl.ds(d1, local), :].astype(F32)).astype(BF16)
-    gsig[pl.ds(local, d1), :] = (loc1[pl.ds(local, d1), :] + back1[...].astype(F32)).astype(BF16)
+    rest = steps - d1
+    if rest:
+        gsig[pl.ds(0, rest), :] = (loc1[pl.ds(0, rest), :] + ahead1[pl.ds(d1, rest), :].astype(F32)).astype(BF16)
+    gsig[pl.ds(rest, d1), :] = (loc1[pl.ds(rest, d1), :] + back1[...].astype(F32)).astype(BF16)
     stores[0].start()
 
     sum_one.send3()
@@ -349,10 +371,10 @@
     sum_one.back3()
     sum_one.back2()
     sum_two.finish()
-    stores[2].start()
+    unpack(out2, 4)
     sum_one.back1()
     sum_one.finish()
-    stores[1].start()
+    unpack(out1, 1)
     sum_one.drain()
     sum_two.drain()
 
@@ -363,9 +385,10 @@
     def _():
         halo_copy.wait_send()
     for i in range(len(chunks)):
-        @pl.when(has_far)
-        def _(i=i):
-            mid_copy[i].wait_send()
+        if i >= len(chunks) - 2:
+            @pl.when(has_far)
+            def _(i=i):
+                mid_copy[i].wait_send()
 
         @pl.when(has_near)
         def _(i=i):
@@ -376,19 +399,17 @@
                 a1_copy[i].wait_send()
 
 
-def write(gs, one, two, gsig, gp1, gn1, gm1, gp2, gn2, gm2, sem):
-    copies = [pltpu.make_async_copy(gs, gsig, sem.at[20])]
-    for k, (packed, outs) in enumerate(((one, (gp1, gn1, gm1)), (two, (gp2, gn2, gm2)))):
-        block = 0
-        for out in outs:
-            height = out.shape[0]
-            for j in range(out.shape[1] // 128):
-                src = packed.at[pl.ds(block * height, height)]
-                copies.append(pltpu.make_async_copy(src, out.at[:, pl.ds(j * 128, 128)], sem.at[k * 10 + block]))
-                block += 1
-    for c in copies:
+def write(*refs):
+    count = len(refs) // 3
+    src, dst, (*held, sem) = refs[:count], refs[count : 2 * count], refs[2 * count :]
+    inward = [pltpu.make_async_copy(a, b, sem.at[0, i]) for i, (a, b) in enumerate(zip(src, held))]
+    outward = [pltpu.make_async_copy(a, b, sem.at[1, i]) for i, (a, b) in enumerate(zip(held, dst))]
+    for c in inward:
         c.start()
-    for c in copies:
+    for a, b in zip(inward, outward):
+        a.wait()
+        b.start()
+    for c in outward:
         c.wait()
 
 
@@ -418,17 +439,20 @@
         dma((14,)),
         dma((14,)),
     ]
-    gs, one, two = pl.pallas_call(
+    kind = packed.dtype
+    shapes = [S((steps, c), BF16)] + [S((c, gate), kind), S((c, gate), kind), S((c, c), kind)] * 2
+    held = [pltpu.VMEM(a.shape, a.dtype) for a in shapes]
+    out = pl.pallas_call(
         functools.partial(kernel, count, SECOND_DILATION // steps, steps, chunks, scale, fused),
-        out_shape=[S((steps, c), BF16), packed, packed],
+        out_shape=shapes,
         in_specs=[hbm] * 8,
-        out_specs=[hbm] * 3,
+        out_specs=[hbm] * 7,
         scratch_shapes=[pltpu.VMEM(a.shape, BF16) for a in args]
         + [
-            pltpu.VMEM((steps, c), BF16),
+            *held,
             pltpu.VMEM(packed.shape, packed.dtype),
             pltpu.VMEM(packed.shape, packed.dtype),
-            dma((3,)),
+            dma((7,)),
             pltpu.VMEM((FIRST_DILATION, c), BF16),
             pltpu.VMEM((steps, c), F32),
             pltpu.VMEM((steps, c), F32),
@@ -453,20 +477,20 @@
         ),
         name="layers",
     )(*args)
-    if not fused:
-        one, two = lax.psum((one, two), ("dp", "tm"))
-        one, two = (one * scale).astype(BF16), (two * scale).astype(BF16)
-    shapes = [S((steps, c), BF16)] + [S((c, gate), BF16), S((c, gate), BF16), S((c, c), BF16)] * 2
-    out = pl.pallas_call(
-        write,
-        out_shape=shapes,
-        in_specs=[hbm] * 3,
-        out_specs=[hbm] * 7,
-        scratch_shapes=[dma((21,))],
-        compiler_params=pltpu.CompilerParams(vmem_limit_bytes=62 * 1024 * 1024),
-        name="write",
-    )(gs, one, two)
-    return (out[0].reshape(signal.shape),) + tuple(out[1:])
+    if fused:
+        out = pl.pallas_call(
+            write,
+            out_shape=shapes,
+            in_specs=[hbm] * 7,
+            out_specs=[hbm] * 7,
+            scratch_shapes=held + [dma((2, 7))],
+            compiler_params=pltpu.CompilerParams(vmem_limit_bytes=62 * 1024 * 1024),
+            name="write",
+        )(*out)
+        grads = tuple(out[1:])
+    else:
+        grads = tuple((t * scale).astype(BF16) for t in lax.psum(tuple(out[1:]), ("dp", "tm")))
+    return (out[0].reshape(signal.shape),) + grads
 
 
 def solution(mesh):

time: 134 us -> 77.7 us (0.58)
  Pallas kernels: 133 us -> 76.9 us
    pallas_call x1, Pallas kernels: 56.9 us -> 2.38 us  [body(): pl.pallas_call(write, out_shape=shapes, in_specs=[hbm] * 7, out_specs=[hb...]
    pallas_call x1, Pallas kernels: 76.1 us -> 74.5 us  [body(): pl.pallas_call(functools.partial(kernel, count, SECOND_DILATION // steps,...]
where the time goes in v3:
time: 77.7 us; the launch traced here: 77.5 us
  Pallas kernels  76.9 us (99%)
    pallas_call x1, Pallas kernels, body(): pl.pallas_call(functools.partial(kernel, count, SECOND_DILATION // steps,...  74.5 us
    pallas_call x1, Pallas kernels, body(): pl.pallas_call(write, out_shape=shapes, in_specs=[hbm] * 7, out_specs=[hb...  2.38 us

profile of v3, /device:TPU:1, one launch (start us, length us, event | category | flops | bytes accessed | tf_op | source)
XLA Modules:
  0.0 77.5 jit_solution(15971281351676126681)
XLA Ops:
  0.6 74.5 %layers.1 = (bf16[1024,256]{1,0:T(8,128)(2,1)}, bf16[256,512]{1,0:T(8,128)(2,1)}, bf16[256,512]{1,0:T(8,128)(2,1)}, bf16[256,256]{1,0:T(8,128)(2,1)}, bf16[256,5...) custom-call(bf16[1024,256]{1,0:T(8,128)(2,1)} %bitcast.3, bf16[1024,256]{1,0:T(8,128)(2,1)} %bitcast.4, ...), custom_call_target="tpu_custom_call" | custom-call | tf_op jit(solution)/shard_map/layers/pallas_call | solution.py:445
  75.1 2.4 %write.1 = (bf16[1024,256]{1,0:T(8,128)(2,1)}, bf16[256,512]{1,0:T(8,128)(2,1)}, bf16[256,512]{1,0:T(8,128)(2,1)}, bf16[256,256]{1,0:T(8,128)(2,1)}, bf16[256,51...) custom-call(bf16[1024,256]{1,0:T(8,128)(2,1)} %get-tuple-element.21.refs_0_, ...), custom_call_target="tpu_custom_call" | custom-call | tf_op jit(solution)/shard_map/write/pallas_call | solution.py:481

commit v4 on v3

--- a/solution.py
+++ b/solution.py
@@ -17,10 +17,6 @@
 
 def mm(a, b):
     return lax.dot_general(a, b, (((1,), (0,)), ((), ())), preferred_element_type=F32)
-
-
-def mm_nt(a, b):
-    return lax.dot_general(a, b, (((1,), (1,)), ((), ())), preferred_element_type=F32)
 
 
 def mm_tn(a, b):
@@ -172,6 +168,8 @@
                 block += 1
             stores[i].start()
     halo, f1, g1, h1, mid, past2, ahead2, back2, pre2, hg2, loc2, ahead1, back1, loc1 = refs[:14]
+    h2, up1, pg1, pg2, sigt, midt, h1t, halot, m2t, p2t, w2t, m1t, p1t, w1t = refs[14:28]
+    refs = refs[:14] + refs[28:]
     load, halo_s, halo_r, mid_s, mid_r, a2_s, a2_r, a1_s, a1_r = refs[14:23]
     sig, cot, p1, w1, m1, p2, w2, m2 = vmem
     loads = {}
@@ -276,10 +274,19 @@
 
     for i in (6, 1, 7, 5):
         loads[i].wait()
+    for weight, turned in ((m2, m2t), (p2, p2t), (w2, w2t), (m1, m1t), (p1, p1t), (w1, w1t)):
+        turned[...] = weight[...].T
     for at, size in chunks:
         rows = pl.ds(at, size)
         pre2[rows, :] = mm(mid[rows, :], w2[...])
-        hg2[rows, :] = mm_nt(cot[rows, :], m2[...])
+        hg2[rows, :] = mm(cot[rows, :], m2t[...])
+    for at, size in chunks:
+        rows = pl.ds(at, size)
+        sigt[:, rows] = sig[rows, :].T
+        midt[:, rows] = mid[rows, :].T
+        h1t[:, rows] = h1[rows, :].T
+        if at < d1:
+            halot[:, rows] = halo[rows, :].T
 
     def second(i):
         at, size = chunks[i]
@@ -288,21 +295,31 @@
         @pl.when(has_near)
         def _():
             mid_copy[i].wait_recv()
-        past = past2[rows, :]
         up = cot[rows, :]
-        pre = mm(past, p2[...]) + pre2[rows, :]
+        pre = mm(past2[rows, :], p2[...]) + pre2[rows, :]
         f = jnp.tanh(pre[:, :c])
         g = sigmoid(pre[:, c:])
-        hid = (f * g).astype(BF16)
+        h2[rows, :] = (f * g).astype(BF16)
         hg = hg2[rows, :]
         pg = jnp.concatenate([hg * g * (1.0 - f * f), hg * f * g * (1.0 - g)], axis=1).astype(BF16)
+        pg2[rows, :] = pg
 
         @pl.when(has_near)
         def _():
-            ahead2[rows, :] = mm_nt(pg, p2[...]).astype(BF16)
+            ahead2[rows, :] = mm(pg, p2t[...]).astype(BF16)
             a2_copy[i].start()
-        loc2[rows, :] = up.astype(F32) + mm_nt(pg, w2[...])
-        sum_two.add(i == 0, mm_tn(past, pg), mm_tn(mid[rows, :], pg), mm_tn(hid, up))
+        loc2[rows, :] = up.astype(F32) + mm(pg, w2t[...])
+
+    def second_terms(at, size, begin):
+        rows = pl.ds(at, size)
+        pg = pg2[rows, :]
+        sum_two.add(begin, None, mm(midt[:, rows], pg), mm_tn(h2[rows, :], cot[rows, :]))
+        if begin:
+            sum_two.acc[pl.ds(0, 4 * c), :] = jnp.zeros((4 * c, 128), F32)
+
+        @pl.when(has_near)
+        def _():
+            sum_two.add(False, mm_tn(past2[rows, :], pg), None, None)
 
     def first(i):
         at, size = chunks[i]
@@ -312,46 +329,55 @@
         def _():
             a2_copy[i].wait_recv()
         up = (loc2[rows, :] + back2[rows, :].astype(F32)).astype(BF16)
-        hg = mm_nt(up, m1[...])
+        up1[rows, :] = up
+        hg = mm(up, m1t[...])
         f, g = f1[rows, :], g1[rows, :]
         pg = jnp.concatenate([hg * g * (1.0 - f * f), hg * f * g * (1.0 - g)], axis=1).astype(BF16)
-        def terms():
-            sum_one.add(i == 0, mm_tn(past1(at, size), pg), mm_tn(sig[rows, :], pg), mm_tn(h1[rows, :], up))
-
-        def grads():
-            ahead1[rows, :] = mm_nt(pg, p1[...]).astype(BF16)
-            if at < d1:
-                @pl.when(has_prev)
-                def _():
-                    a1_copy[i].start()
-            loc1[rows, :] = up.astype(F32) + mm_nt(pg, w1[...])
-
-        if i < last:
-            grads()
-            terms()
-        else:
-            terms()
-            sum_one.send1()
-            grads()
-
-    last = len(chunks) - 1
+        pg1[rows, :] = pg
+
+    def first_grads(i):
+        at, size = chunks[i]
+        rows = pl.ds(at, size)
+        pg = pg1[rows, :]
+        ahead1[rows, :] = mm(pg, p1t[...]).astype(BF16)
+        if at < d1:
+            @pl.when(has_prev)
+            def _():
+                a1_copy[i].start()
+        loc1[rows, :] = up1[rows, :].astype(F32) + mm(pg, w1t[...])
+
+    def first_terms(at, size, begin):
+        rows = pl.ds(at, size)
+        past = halot[:, rows] if at < d1 else sigt[:, pl.ds(at - d1, size)]
+        pg = pg1[rows, :]
+        sum_one.add(begin, mm(past, pg), mm(sigt[:, rows], pg), mm(h1t[:, rows], up1[rows, :]))
+
+    span = chunks[1][1]
     second(0)
     send_middle(2)
     second(1)
     send_middle(3)
+    second_terms(d1, span, True)
+    first(0)
+    first_grads(0)
     second(2)
-    send_middle(4)
-    first(0)
+    second_terms(0, d1, False)
+    first(1)
+    first_grads(1)
     second(3)
-    first(1)
-    second(4)
+    second_terms(d1 + span, span, False)
     sum_two.send1()
+    first_terms(d1, span, True)
     first(2)
+    first_grads(2)
     sum_two.send2()
-    first(last - 1)
+    first_terms(0, d1, False)
     sum_two.send3()
-    first(last)
+    first(3)
+    first_terms(d1 + span, span, False)
+    sum_one.send1()
     sum_two.back3()
+    first_grads(3)
     sum_one.send2()
     sum_two.back2()
 
@@ -419,7 +445,7 @@
     gate = p1.shape[1]
     scale = 1.0 / math.sqrt(seqs * groups * steps * count)
     fused = (groups, count) == (2, 16)
-    chunks = ((512, 256), (0, 256), (256, 256), (768, 128), (896, 128))
+    chunks = ((512, 256), (0, 256), (256, 256), (768, 256))
     nch = len(chunks)
     hbm = pl.BlockSpec(memory_space=pltpu.HBM)
     S = jax.ShapeDtypeStruct
@@ -467,6 +493,15 @@
             pltpu.VMEM((steps, c), BF16),
             pltpu.VMEM((FIRST_DILATION, c), BF16),
             pltpu.VMEM((steps, c), F32),
+            pltpu.VMEM((steps, c), BF16),
+            pltpu.VMEM((steps, c), BF16),
+            pltpu.VMEM((steps, gate), BF16),
+            pltpu.VMEM((steps, gate), BF16),
+            pltpu.VMEM((c, steps), BF16),
+            pltpu.VMEM((c, steps), BF16),
+            pltpu.VMEM((c, steps), BF16),
+            pltpu.VMEM((c, FIRST_DILATION), BF16),
+            *[pltpu.VMEM((n, c), BF16) for n in (c, gate, gate, c, gate, gate)],
             dma((8,)),
             dma, dma,
             dma((nch,)), dma((nch,)), dma((nch,)), dma((nch,)), dma((nch,)), dma((nch,)),

time: 77.7 us -> 78 us (level)
  no operation moved by 1% of the time
where the time goes in v4:
time: 78 us; the launch traced here: 77.8 us
  Pallas kernels  77.2 us (99%)
    pallas_call x1, Pallas kernels, body(): pl.pallas_call(functools.partial(kernel, count, SECOND_DILATION // steps,...  74.8 us
    pallas_call x1, Pallas kernels, body(): pl.pallas_call(write, out_shape=shapes, in_specs=[hbm] * 7, out_specs=[hb...  2.38 us

profile of v4, /device:TPU:1, one launch (start us, length us, event | category | flops | bytes accessed | tf_op | source)
XLA Modules:
  0.0 77.8 jit_solution(2988217524847056533)
XLA Ops:
  0.6 74.8 %layers.1 = (bf16[1024,256]{1,0:T(8,128)(2,1)}, bf16[256,512]{1,0:T(8,128)(2,1)}, bf16[256,512]{1,0:T(8,128)(2,1)}, bf16[256,256]{1,0:T(8,128)(2,1)}, bf16[256,5...) custom-call(bf16[1024,256]{1,0:T(8,128)(2,1)} %bitcast.3, bf16[1024,256]{1,0:T(8,128)(2,1)} %bitcast.4, ...), custom_call_target="tpu_custom_call" | custom-call | tf_op jit(solution)/shard_map/layers/pallas_call | solution.py:471
  75.4 2.4 %write.1 = (bf16[1024,256]{1,0:T(8,128)(2,1)}, bf16[256,512]{1,0:T(8,128)(2,1)}, bf16[256,512]{1,0:T(8,128)(2,1)}, bf16[256,256]{1,0:T(8,128)(2,1)}, bf16[256,51...) custom-call(bf16[1024,256]{1,0:T(8,128)(2,1)} %get-tuple-element.21.refs_0_, ...), custom_call_target="tpu_custom_call" | custom-call | tf_op jit(solution)/shard_map/write/pallas_call | solution.py:516

commit v5 on v4

--- a/solution.py
+++ b/solution.py
@@ -17,6 +17,10 @@
 
 def mm(a, b):
     return lax.dot_general(a, b, (((1,), (0,)), ((), ())), preferred_element_type=F32)
+
+
+def mm_nt(a, b):
+    return lax.dot_general(a, b, (((1,), (1,)), ((), ())), preferred_element_type=F32)
 
 
 def mm_tn(a, b):
@@ -168,8 +172,8 @@
                 block += 1
             stores[i].start()
     halo, f1, g1, h1, mid, past2, ahead2, back2, pre2, hg2, loc2, ahead1, back1, loc1 = refs[:14]
-    h2, up1, pg1, pg2, sigt, midt, h1t, halot, m2t, p2t, w2t, m1t, p1t, w1t = refs[14:28]
-    refs = refs[:14] + refs[28:]
+    h2, up1, pg1, pg2 = refs[14:18]
+    refs = refs[:14] + refs[18:]
     load, halo_s, halo_r, mid_s, mid_r, a2_s, a2_r, a1_s, a1_r = refs[14:23]
     sig, cot, p1, w1, m1, p2, w2, m2 = vmem
     loads = {}
@@ -274,20 +278,10 @@
 
     for i in (6, 1, 7, 5):
         loads[i].wait()
-    for weight, turned in ((m2, m2t), (p2, p2t), (w2, w2t), (m1, m1t), (p1, p1t), (w1, w1t)):
-        turned[...] = weight[...].T
     for at, size in chunks:
         rows = pl.ds(at, size)
         pre2[rows, :] = mm(mid[rows, :], w2[...])
-        hg2[rows, :] = mm(cot[rows, :], m2t[...])
-    for at, size in chunks:
-        rows = pl.ds(at, size)
-        sigt[:, rows] = sig[rows, :].T
-        midt[:, rows] = mid[rows, :].T
-        h1t[:, rows] = h1[rows, :].T
-        if at < d1:
-            halot[:, rows] = halo[rows, :].T
-
+        hg2[rows, :] = mm_nt(cot[rows, :], m2[...])
     def second(i):
         at, size = chunks[i]
         rows = pl.ds(at, size)
@@ -306,14 +300,14 @@
 
         @pl.when(has_near)
         def _():
-            ahead2[rows, :] = mm(pg, p2t[...]).astype(BF16)
+            ahead2[rows, :] = mm_nt(pg, p2[...]).astype(BF16)
             a2_copy[i].start()
-        loc2[rows, :] = up.astype(F32) + mm(pg, w2t[...])
+        loc2[rows, :] = up.astype(F32) + mm_nt(pg, w2[...])
 
     def second_terms(at, size, begin):
         rows = pl.ds(at, size)
         pg = pg2[rows, :]
-        sum_two.add(begin, None, mm(midt[:, rows], pg), mm_tn(h2[rows, :], cot[rows, :]))
+        sum_two.add(begin, None, mm_tn(mid[rows, :], pg), mm_tn(h2[rows, :], cot[rows, :]))
         if begin:
             sum_two.acc[pl.ds(0, 4 * c), :] = jnp.zeros((4 * c, 128), F32)
 
@@ -330,7 +324,7 @@
             a2_copy[i].wait_recv()
         up = (loc2[rows, :] + back2[rows, :].astype(F32)).astype(BF16)
         up1[rows, :] = up
-        hg = mm(up, m1t[...])
+        hg = mm_nt(up, m1[...])
         f, g = f1[rows, :], g1[rows, :]
         pg = jnp.concatenate([hg * g * (1.0 - f * f), hg * f * g * (1.0 - g)], axis=1).astype(BF16)
         pg1[rows, :] = pg
@@ -339,46 +333,45 @@
         at, size = chunks[i]
         rows = pl.ds(at, size)
         pg = pg1[rows, :]
-        ahead1[rows, :] = mm(pg, p1t[...]).astype(BF16)
+        ahead1[rows, :] = mm_nt(pg, p1[...]).astype(BF16)
         if at < d1:
             @pl.when(has_prev)
             def _():
                 a1_copy[i].start()
-        loc1[rows, :] = up1[rows, :].astype(F32) + mm(pg, w1t[...])
+        loc1[rows, :] = up1[rows, :].astype(F32) + mm_nt(pg, w1[...])
 
     def first_terms(at, size, begin):
         rows = pl.ds(at, size)
-        past = halot[:, rows] if at < d1 else sigt[:, pl.ds(at - d1, size)]
         pg = pg1[rows, :]
-        sum_one.add(begin, mm(past, pg), mm(sigt[:, rows], pg), mm(h1t[:, rows], up1[rows, :]))
+        sum_one.add(begin, mm_tn(past1(at, size), pg), mm_tn(sig[rows, :], pg), mm_tn(h1[rows, :], up1[rows, :]))
 
     span = chunks[1][1]
     second(0)
     send_middle(2)
     second(1)
     send_middle(3)
-    second_terms(d1, span, True)
     first(0)
     first_grads(0)
     second(2)
-    second_terms(0, d1, False)
+    second_terms(d1, span, True)
     first(1)
     first_grads(1)
     second(3)
+    second_terms(0, d1, False)
     second_terms(d1 + span, span, False)
     sum_two.send1()
     first_terms(d1, span, True)
     first(2)
+    sum_two.send2()
     first_grads(2)
-    sum_two.send2()
     first_terms(0, d1, False)
-    sum_two.send3()
     first(3)
     first_terms(d1 + span, span, False)
     sum_one.send1()
-    sum_two.back3()
+    sum_two.send3()
     first_grads(3)
     sum_one.send2()
+    sum_two.back3()
     sum_two.back2()
 
     for i, (at, size) in enumerate(chunks):
@@ -497,11 +490,6 @@
             pltpu.VMEM((steps, c), BF16),
             pltpu.VMEM((steps, gate), BF16),
             pltpu.VMEM((steps, gate), BF16),
-            pltpu.VMEM((c, steps), BF16),
-            pltpu.VMEM((c, steps), BF16),
-            pltpu.VMEM((c, steps), BF16),
-            pltpu.VMEM((c, FIRST_DILATION), BF16),
-            *[pltpu.VMEM((n, c), BF16) for n in (c, gate, gate, c, gate, gate)],
             dma((8,)),
             dma, dma,
             dma((nch,)), dma((nch,)), dma((nch,)), dma((nch,)), dma((nch,)), dma((nch,)),

time: 78 us -> 77.5 us (level)
  no operation moved by 1% of the time
where the time goes in v5:
time: 77.5 us; the launch traced here: 77.3 us
  Pallas kernels  76.7 us (99%)
    pallas_call x1, Pallas kernels, body(): pl.pallas_call(functools.partial(kernel, count, SECOND_DILATION // steps,...  74.3 us
    pallas_call x1, Pallas kernels, body(): pl.pallas_call(write, out_shape=shapes, in_specs=[hbm] * 7, out_specs=[hb...  2.38 us

profile of v5, /device:TPU:1, one launch (start us, length us, event | category | flops | bytes accessed | tf_op | source)
XLA Modules:
  0.0 77.3 jit_solution(17764037198966106271)
XLA Ops:
  0.6 74.3 %layers.1 = (bf16[1024,256]{1,0:T(8,128)(2,1)}, bf16[256,512]{1,0:T(8,128)(2,1)}, bf16[256,512]{1,0:T(8,128)(2,1)}, bf16[256,256]{1,0:T(8,128)(2,1)}, bf16[256,5...) custom-call(bf16[1024,256]{1,0:T(8,128)(2,1)} %bitcast.3, bf16[1024,256]{1,0:T(8,128)(2,1)} %bitcast.4, ...), custom_call_target="tpu_custom_call" | custom-call | tf_op jit(solution)/shard_map/layers/pallas_call | solution.py:464
  74.9 2.4 %write.1 = (bf16[1024,256]{1,0:T(8,128)(2,1)}, bf16[256,512]{1,0:T(8,128)(2,1)}, bf16[256,512]{1,0:T(8,128)(2,1)}, bf16[256,256]{1,0:T(8,128)(2,1)}, bf16[256,51...) custom-call(bf16[1024,256]{1,0:T(8,128)(2,1)} %get-tuple-element.21.refs_0_, ...), custom_call_target="tpu_custom_call" | custom-call | tf_op jit(solution)/shard_map/write/pallas_call | solution.py:504

commit v6 on v5

--- a/solution.py
+++ b/solution.py
@@ -352,27 +352,30 @@
     send_middle(3)
     first(0)
     first_grads(0)
+    second_terms(d1, 2 * span, True)
     second(2)
-    second_terms(d1, span, True)
     first(1)
     first_grads(1)
+    second_terms(0, span, False)
     second(3)
-    second_terms(0, d1, False)
-    second_terms(d1 + span, span, False)
+    second_terms(span, span, False)
     sum_two.send1()
-    first_terms(d1, span, True)
     first(2)
+    first_grads(2)
     sum_two.send2()
-    first_grads(2)
-    first_terms(0, d1, False)
+    first_terms(d1, 2 * span, True)
+    first_terms(0, span, False)
     first(3)
-    first_terms(d1 + span, span, False)
+    first_terms(span, span, False)
     sum_one.send1()
     sum_two.send3()
     first_grads(3)
     sum_one.send2()
     sum_two.back3()
     sum_two.back2()
+    sum_one.send3()
+    sum_two.back1()
+    sum_one.back3()
 
     for i, (at, size) in enumerate(chunks):
         if at < d1:
@@ -385,9 +388,6 @@
     gsig[pl.ds(rest, d1), :] = (loc1[pl.ds(rest, d1), :] + back1[...].astype(F32)).astype(BF16)
     stores[0].start()
 
-    sum_one.send3()
-    sum_two.back1()
-    sum_one.back3()
     sum_one.back2()
     sum_two.finish()
     unpack(out2, 4)
@@ -438,7 +438,7 @@
     gate = p1.shape[1]
     scale = 1.0 / math.sqrt(seqs * groups * steps * count)
     fused = (groups, count) == (2, 16)
-    chunks = ((512, 256), (0, 256), (256, 256), (768, 256))
+    chunks = ((512, 256), (768, 256), (0, 256), (256, 256))
     nch = len(chunks)
     hbm = pl.BlockSpec(memory_space=pltpu.HBM)
     S = jax.ShapeDtypeStruct

time: 77.5 us -> 78.6 us (1.014)
  Pallas kernels: 76.7 us -> 77.8 us
    pallas_call x1, Pallas kernels: 74.3 us -> 75.5 us  [body(): pl.pallas_call(functools.partial(kernel, count, SECOND_DILATION // steps,...]
where the time goes in v6:
time: 78.6 us; the launch traced here: 78.5 us
  Pallas kernels  77.8 us (99%)
    pallas_call x1, Pallas kernels, body(): pl.pallas_call(functools.partial(kernel, count, SECOND_DILATION // steps,...  75.5 us
    pallas_call x1, Pallas kernels, body(): pl.pallas_call(write, out_shape=shapes, in_specs=[hbm] * 7, out_specs=[hb...  2.38 us

profile of v6, /device:TPU:1, one launch (start us, length us, event | category | flops | bytes accessed | tf_op | source)
XLA Modules:
  0.0 78.5 jit_solution(12257457357319641629)
XLA Ops:
  0.6 75.5 %layers.1 = (bf16[1024,256]{1,0:T(8,128)(2,1)}, bf16[256,512]{1,0:T(8,128)(2,1)}, bf16[256,512]{1,0:T(8,128)(2,1)}, bf16[256,256]{1,0:T(8,128)(2,1)}, bf16[256,5...) custom-call(bf16[1024,256]{1,0:T(8,128)(2,1)} %bitcast.3, bf16[1024,256]{1,0:T(8,128)(2,1)} %bitcast.4, ...), custom_call_target="tpu_custom_call" | custom-call | tf_op jit(solution)/shard_map/layers/pallas_call | solution.py:464
  76.1 2.4 %write.1 = (bf16[1024,256]{1,0:T(8,128)(2,1)}, bf16[256,512]{1,0:T(8,128)(2,1)}, bf16[256,512]{1,0:T(8,128)(2,1)}, bf16[256,256]{1,0:T(8,128)(2,1)}, bf16[256,51...) custom-call(bf16[1024,256]{1,0:T(8,128)(2,1)} %get-tuple-element.21.refs_0_, ...), custom_call_target="tpu_custom_call" | custom-call | tf_op jit(solution)/shard_map/write/pallas_call | solution.py:504
